TPU v7x, 32 devices: a whole 2x2x4 slice. The times are simulated.
32 devices in a mesh: row: 4 (over z), col: 4 (over y, core), depth: 2 (over x).
Axes of the slice: x: 2, y: 2, z: 4, core: 2. Of those that a mesh axis runs over, the one named last changes fastest.
Arguments:
- tokens: bfloat16 [768, 12288], P(('col', 'depth'), 'row'), may hold values from -6 to 6
- w_up: bfloat16 [12288, 24576], P(('row', 'depth'), 'col'), may hold values from -0.0546875 to 0.0546875
- w_down: bfloat16 [24576, 12288], P('col', ('row', 'depth')), may hold values from -0.0390625 to 0.0390625
- cotangent: bfloat16 [768, 12288], P(('col', 'depth'), 'row'), may hold values from -6 to 6
Outputs:
- output: bfloat16 [768, 12288], P(('col', 'depth'), 'row')
- grad_tokens: bfloat16 [768, 12288], P(('col', 'depth'), 'row')
- grad_up: bfloat16 [12288, 24576], P(('row', 'depth'), 'col')
- grad_down: bfloat16 [24576, 12288], P('col', ('row', 'depth'))
All inputs are finite; a program needn't handle non-finite values.
Results may differ from a plain program's by a relative error of at most 0.0059.
Values may be sent and summed in bfloat16 or wider, within the bound.
A program may use at most 384 MiB of HBM per device.

v0:
```python
import math

import jax
import jax.numpy as jnp
from jax import lax
from jax.sharding import PartitionSpec as P

root_coeff = math.sqrt(2.0 / math.pi)


def gelu_pair(pre_act):
    inner_arg = root_coeff * (pre_act + 0.044715 * pre_act * pre_act * pre_act)
    tangent = jnp.tanh(inner_arg)
    gelu_value = 0.5 * pre_act * (1.0 + tangent)
    gelu_slope = 0.5 * (1.0 + tangent) + 0.5 * pre_act * (1.0 - tangent * tangent) * root_coeff * (
        1.0 + 0.134145 * pre_act * pre_act
    )
    return (gelu_value, gelu_slope)


def rounded(partial_grad):
    return lax.optimization_barrier(partial_grad.astype(jnp.bfloat16)).astype(jnp.float32)


def row_product(left_rows, right_side):
    return jnp.dot(left_rows, right_side, preferred_element_type=jnp.float32)


def row_product_t(left_rows, right_side):
    return lax.dot_general(
        left_rows, right_side, (((1,), (1,)), ((), ())), preferred_element_type=jnp.float32
    )


def body(tokens, w_up, w_down, cotangent):
    depth_at = lax.axis_index("depth")
    n_depth = lax.axis_size("depth")
    n_cols = lax.axis_size("col")
    half_width = w_up.shape[0]
    x_all = lax.all_gather(tokens, ("col", "depth"), axis=0, tiled=True)
    x_sub = lax.dynamic_slice_in_dim(x_all, depth_at * half_width, half_width, 1)
    row_total = x_all.shape[0]
    pre_act = lax.psum_scatter(
        row_product(x_sub, w_up), ("row", "depth"), scatter_dimension=0, tiled=True
    )
    gelu_value, gelu_slope = gelu_pair(pre_act)
    hidden = gelu_value.astype(jnp.bfloat16)
    hidden_all = lax.all_gather(hidden, ("row", "depth"), axis=0, tiled=True)
    out_cols = lax.psum_scatter(
        row_product(hidden_all, w_down), "col", scatter_dimension=0, tiled=True
    ).astype(jnp.bfloat16)
    output = lax.all_to_all(out_cols, "depth", split_axis=0, concat_axis=1, tiled=True)
    cot_all = lax.all_gather(cotangent, ("col", "depth"), axis=0, tiled=True)
    cot_sub = lax.dynamic_slice_in_dim(cot_all, depth_at * half_width, half_width, 1)
    d_hidden = lax.psum_scatter(
        row_product_t(cot_sub, w_down), ("row", "depth"), scatter_dimension=0, tiled=True
    )
    d_pre = (d_hidden * gelu_slope).astype(jnp.bfloat16)
    dpre_all = lax.all_gather(d_pre, ("row", "depth"), axis=0, tiled=True)
    dx_cols = lax.psum_scatter(
        row_product_t(dpre_all, w_up), "col", scatter_dimension=0, tiled=True
    ).astype(jnp.bfloat16)
    grad_tokens = lax.all_to_all(dx_cols, "depth", split_axis=0, concat_axis=1, tiled=True)
    block = row_total // (n_cols * n_depth)

    def depth_grad(left_side, right_side):
        left_parts = left_side.reshape(n_cols, n_depth, block, left_side.shape[1])
        right_parts = right_side.reshape(n_cols, n_depth, block, right_side.shape[1])
        accum = jnp.zeros((left_side.shape[1], right_side.shape[1]), jnp.float32)
        for index_depth in range(n_depth):
            left_rows = left_parts[:, index_depth].reshape(-1, left_side.shape[1])
            right_rows = right_parts[:, index_depth].reshape(-1, right_side.shape[1])
            accum = accum + rounded(
                lax.dot_general(
                    left_rows,
                    right_rows,
                    (((0,), (0,)), ((), ())),
                    preferred_element_type=jnp.float32,
                )
            )
        return accum.astype(jnp.bfloat16)

    grad_up = depth_grad(x_sub, dpre_all)
    grad_down = depth_grad(hidden_all, cot_sub)
    return (output, grad_tokens, grad_up, grad_down)


def solution(mesh):
    placed = (
        P(("col", "depth"), "row"),
        P(("row", "depth"), "col"),
        P("col", ("row", "depth")),
        P(("col", "depth"), "row"),
    )
    return jax.shard_map(
        body,
        mesh=mesh,
        in_specs=placed,
        out_specs=(
            P(("col", "depth"), "row"),
            P(("col", "depth"), "row"),
            P(("row", "depth"), "col"),
            P("col", ("row", "depth")),
        ),
        check_vma=False,
    )
```

profile of v0, /device:TPU:0, one launch (start us, length us, event | category | flops | bytes accessed | tf_op | source)
XLA Modules:
  0.0 1143.7 jit_solution(777746637123550192)
XLA Ops:
  7.2 0.0 all-gather.9.cloned.1.call-start
  7.2 0.7 all-gather.9.cloned.1.call-update
  7.9 0.0 all-gather.5.cloned.1.call-start
  7.9 0.7 all-gather.5.cloned.1.call-update
  8.6 0.0 reduce-scatter.9.cloned.1.call-start
  8.7 42.8 %all-gather.9.cloned.1.call-done = bf16[768,3072]{1,0:T(8,128)(2,1)} async-done(((bf16[96,3072]{1,0:T(8,128)(2,1)}), bf16[768,3072]{1,0:T(8,128)(2,1)}) %all-gather.9.cloned.1.call-update) | async-done | bytes 4718608 | tf_op jit(solution)/shard_map/all_gather | solution.py:53
  51.5 1.8 constant_dynamic-slice_fusion
  53.3 0.0 copy-start
  53.4 1.4 copy-done
  54.7 20.7 %fusion.9 = f32[768,6144]{1,0:T(8,128)} fusion(bf16[768,1536]{1,0:T(8,128)(2,1)S(1)} %constant_dynamic-slice_fusion, bf16[6144,1536]{1,0:T(8,128)(2,1)} %param.6), kind=kOutput, calls=%fused_computation.28 | convolution fusion | flops 14495514624 | bytes 40108032 | tf_op jit(solution)/shard_map/dot_general | solution.py:30
  75.5 0.0 reduce-scatter.9.cloned.1.call-update
  75.5 0.0 reduce-scatter.5.cloned.1.call-start
  75.5 16.8 %all-gather.5.cloned.1.call-done = bf16[768,3072]{1,0:T(8,128)(2,1)} async-done(((bf16[96,3072]{1,0:T(8,128)(2,1)}), bf16[768,3072]{1,0:T(8,128)(2,1)}) %all-gather.5.cloned.1.call-update) | async-done | bytes 4718608 | tf_op jit(solution)/shard_map/all_gather | solution.py:40
  92.4 1.8 constant_dynamic-slice_fusion.1
  94.2 20.7 %fusion.7 = f32[768,6144]{1,0:T(8,128)} fusion(bf16[768,1536]{1,0:T(8,128)(2,1)S(1)} %constant_dynamic-slice_fusion.1, bf16[1536,6144]{1,0:T(8,128)(2,1)} %param.5), kind=kOutput, calls=%fused_computation.26 | convolution fusion | flops 14495514624 | bytes 40108032 | tf_op jit(solution)/shard_map/dot_general | solution.py:26
  114.9 0.0 reduce-scatter.5.cloned.1.call-update
  114.9 0.0 all-gather.7.cloned.1.call-start
  115.0 294.7 %reduce-scatter.9.cloned.1.call-done = f32[96,6144]{1,0:T(8,128)} async-done(((f32[768,6144]{1,0:T(8,128)}), f32[96,6144]{1,0:T(8,128)}) %reduce-scatter.9.cloned.1.call-update) | async-done | bytes 2359312 | tf_op jit(solution)/shard_map/reduce_scatter | solution.py:55
  409.7 316.7 %reduce-scatter.5.cloned.1.call-done = f32[96,6144]{1,0:T(8,128)} async-done(((f32[768,6144]{1,0:T(8,128)}), f32[96,6144]{1,0:T(8,128)}) %reduce-scatter.5.cloned.1.call-update) | async-done | bytes 2359312 | tf_op jit(solution)/shard_map/reduce_scatter | solution.py:43
  726.4 4.3 fusion.6
  730.6 0.0 all-gather.7.cloned.1.call-update
  730.7 0.0 all-gather.11.cloned.1.call-start
  730.7 0.5 all-gather.11.cloned.1.call-update
  731.2 0.0 reduce-scatter.7.cloned.1.call-start
  731.3 136.7 %all-gather.7.cloned.1.call-done = bf16[768,6144]{1,0:T(8,128)(2,1)} async-done(((bf16[96,6144]{1,0:T(8,128)(2,1)}), bf16[768,6144]{1,0:T(8,128)(2,1)}) %all-gather.7.cloned.1.call-update) | async-done | bytes 9437200 | tf_op jit(solution)/shard_map/all_gather | solution.py:48
  868.0 21.1 %fusion.8 = f32[768,1536]{1,0:T(8,128)} fusion(bf16[768,6144]{1,0:T(8,128)(2,1)} %all-gather.7.cloned.1.call-done, bf16[6144,1536]{1,0:T(8,128)(2,1)} %param.6), kind=kOutput, calls=%fused_computation.27 | convolution fusion | flops 14495514624 | bytes 33030144 | tf_op jit(solution)/shard_map/dot_general | solution.py:26
  889.1 0.0 reduce-scatter.7.cloned.1.call-update
  889.1 0.2 reduce-scatter.11.cloned.1.call-start
  889.4 16.0 %bitcast_convert_fusion.1 = bf16[6144,1536]{1,0:T(8,128)(2,1)} fusion(bf16[4,2,96,6144]{3,2,1,0:T(8,128)(2,1)} %bitcast.78, bf16[4,2,96,1536]{3,2,1,0:T(8,128)(2,1)} %bitcast.70), kind=kOutput, calls=%fused_computation.1 | convolution fusion | flops 7257194496 | bytes 24772608 | tf_op jit(solution)/shard_map/dot_general | solution.py:74
  905.4 101.5 %all-gather.11.cloned.1.call-done = bf16[768,6144]{1,0:T(8,128)(2,1)} async-done(((bf16[96,6144]{1,0:T(8,128)(2,1)}), bf16[768,6144]{1,0:T(8,128)(2,1)}) %all-gather.11.cloned.1.call-update) | async-done | bytes 9437200 | tf_op jit(solution)/shard_map/all_gather | solution.py:59
  1006.9 21.2 %fusion.10 = f32[768,1536]{1,0:T(8,128)} fusion(bf16[768,6144]{1,0:T(8,128)(2,1)} %all-gather.11.cloned.1.call-done, bf16[1536,6144]{1,0:T(8,128)(2,1)} %param.5), kind=kOutput, calls=%fused_computation.29 | convolution fusion | flops 14495514624 | bytes 33030144 | tf_op jit(solution)/shard_map/dot_general | solution.py:30
  1028.2 0.0 reduce-scatter.11.cloned.1.call-update
  1028.2 16.2 %bitcast_convert_fusion = bf16[6144,1536]{1,0:T(8,128)(2,1)} fusion(bf16[4,2,96,6144]{3,2,1,0:T(8,128)(2,1)} %bitcast.79, bf16[4,2,96,1536]{3,2,1,0:T(8,128)(2,1)} %bitcast.71), kind=kOutput, calls=%fused_computation | convolution fusion | flops 7257194496 | bytes 24772608 | tf_op jit(solution)/shard_map/dot_general | solution.py:74
  1044.4 15.4 %bitcast_convert_fusion.3 = bf16[1536,6144]{1,0:T(8,128)(2,1)} fusion(bf16[4,2,96,6144]{3,2,1,0:T(8,128)(2,1)} %bitcast.76, bf16[4,2,96,1536]{3,2,1,0:T(8,128)(2,1)S(1)} %bitcast.68), kind=kOutput, calls=%fused_computation.3 | convolution fusion | flops 7257194496 | bytes 24772608 | tf_op jit(solution)/shard_map/dot_general | solution.py:74
  1059.8 22.4 %add_convert_fusion = bf16[6144,1536]{1,0:T(8,128)(2,1)} fusion(bf16[6144,1536]{1,0:T(8,128)(2,1)} %bitcast_convert_fusion, bf16[6144,1536]{1,0:T(8,128)(2,1)} %bitcast_convert_fusion.1), kind=kLoop, calls=%fused_computation.4 | loop fusion | flops 37748736 | bytes 56623104 | tf_op jit(solution)/shard_map/convert_element_type | solution.py:81
  1082.2 0.0 reduce-scatter.7.cloned.1.call-done
  1082.2 2.1 convert_element_type.43
  1084.4 3.5 all-to-all-start
  1087.9 15.5 %bitcast_convert_fusion.2 = bf16[1536,6144]{1,0:T(8,128)(2,1)} fusion(bf16[4,2,96,6144]{3,2,1,0:T(8,128)(2,1)} %bitcast.77, bf16[4,2,96,1536]{3,2,1,0:T(8,128)(2,1)S(1)} %bitcast.69), kind=kOutput, calls=%fused_computation.2 | convolution fusion | flops 7257194496 | bytes 24772608 | tf_op jit(solution)/shard_map/dot_general | solution.py:74
  1103.4 2.7 reduce-scatter.11.cloned.1.call-done
  1106.1 2.1 convert_element_type.45
  1108.2 0.0 all-to-all-done
  1108.2 3.5 all-to-all-start.1
  1111.7 23.4 %add_convert_fusion.1 = bf16[1536,6144]{1,0:T(8,128)(2,1)} fusion(bf16[1536,6144]{1,0:T(8,128)(2,1)} %bitcast_convert_fusion.2, bf16[1536,6144]{1,0:T(8,128)(2,1)} %bitcast_convert_fusion.3), kind=kLoop, calls=%fused_computation.5 | loop fusion | flops 37748736 | bytes 56623104 | tf_op jit(solution)/shard_map/convert_element_type | solution.py:81
  1135.1 0.9 copy.32
  1136.0 0.0 all-to-all-done.1
  1136.0 0.9 copy.33
Async XLA Ops:
  7.2 44.4 %all-gather.9.cloned.1.call-start = ((), (), s32[]{:S(2)}) async-start(), calls=%async_computation.10 | async-start | bytes 5308416 | tf_op jit(solution)/shard_map/all_gather | solution.py:53
  7.9 84.5 %all-gather.5.cloned.1.call-start = ((), (), s32[]{:S(2)}) async-start(), calls=%async_computation.6 | async-start | bytes 5308416 | tf_op jit(solution)/shard_map/all_gather | solution.py:40
  8.6 401.0 %reduce-scatter.9.cloned.1.call-start = ((), (), s32[]{:S(2)}) async-start(), calls=%async_computation.11 | async-start | bytes 21233664 | tf_op jit(solution)/shard_map/reduce_scatter | solution.py:55
  53.3 1.4 copy-start
  75.5 650.9 %reduce-scatter.5.cloned.1.call-start = ((), (), s32[]{:S(2)}) async-start(), calls=%async_computation.7 | async-start | bytes 21233664 | tf_op jit(solution)/shard_map/reduce_scatter | solution.py:43
  114.9 753.1 %all-gather.7.cloned.1.call-start = ((), (), s32[]{:S(2)}) async-start(), calls=%async_computation.8 | async-start | bytes 10616832 | tf_op jit(solution)/shard_map/all_gather | solution.py:48
  730.7 276.3 %all-gather.11.cloned.1.call-start = ((), (), s32[]{:S(2)}) async-start(), calls=%async_computation.12 | async-start | bytes 10616832 | tf_op jit(solution)/shard_map/all_gather | solution.py:59
  731.2 351.0 %reduce-scatter.7.cloned.1.call-start = ((), (), s32[]{:S(2)}) async-start(), calls=%async_computation.9 | async-start | bytes 5898240 | tf_op jit(solution)/shard_map/reduce_scatter | solution.py:49
  889.1 216.9 %reduce-scatter.11.cloned.1.call-start = ((), (), s32[]{:S(2)}) async-start(), calls=%async_computation.13 | async-start | bytes 5898240 | tf_op jit(solution)/shard_map/reduce_scatter | solution.py:60
  1084.4 23.9 %all-to-all-start = ((bf16[2,96,1536]{2,1,0:T(8,128)(2,1)}), bf16[2,96,1536]{2,1,0:T(8,128)(2,1)S(1)}, u32[]{:S(2)}, u32[]{:S(2)}) async-start(bf16[2,96,1536]{2,1,0:T(8,128)(2,1)} %bitcast), calls=%async_computation.2 | async-start | bytes 1179648 | tf_op jit(solution)/shard_map/all_to_all | solution.py:52
  1108.2 27.8 %all-to-all-start.1 = ((bf16[2,96,1536]{2,1,0:T(8,128)(2,1)}), bf16[2,96,1536]{2,1,0:T(8,128)(2,1)S(1)}, u32[]{:S(2)}, u32[]{:S(2)}) async-start(bf16[2,96,1536]{2,1,0:T(8,128)(2,1)} %bitcast.2), calls=%async_computation.5 | async-start | bytes 1179648 | tf_op jit(solution)/shard_map/all_to_all | solution.py:63
Sparse Core Ops, SparseCore 0:
  9.9 41.6 all-gather.8
  53.4 38.9 all-gather.4
  96.8 312.8 reduce-scatter.8
  414.0 312.3 reduce-scatter.4
  730.8 137.2 all-gather.6
  870.6 136.2 all-gather.10
  1009.5 46.0 reduce-scatter.6
  1058.2 47.8 reduce-scatter.10
where the time goes:
time: 1140 us
  waiting for transfers between devices  914 us (80%)
  matrix products  147 us (13%)
  other arithmetic  54.4 us (5%)
  between operations  14.2 us (1%)
    reduce_scatter x1, waiting for transfers between devices, body(): lax.psum_scatter(row_product(x_sub, w_up), ('row', 'depth'), scatter_dime...  317 us
    reduce_scatter x1, waiting for transfers between devices, body(): lax.psum_scatter(row_product_t(cot_sub, w_down), ('row', 'depth'), scatte...  295 us
    all_gather x1, waiting for transfers between devices, body(): hidden_all = lax.all_gather(hidden, ('row', 'depth'), axis=0, tiled=True)  137 us
    all_gather x1, waiting for transfers between devices, body(): dpre_all = lax.all_gather(d_pre, ('row', 'depth'), axis=0, tiled=True)  102 us
    dot_general x4, matrix products, depth_grad(): lax.dot_general(left_rows, right_rows, (((0,), (0,)), ((), ())), preferre...  63.1 us
    convert_element_type x2, other arithmetic, depth_grad(): return accum.astype(jnp.bfloat16)  45.8 us
    all_gather x1, waiting for transfers between devices, body(): cot_all = lax.all_gather(cotangent, ('col', 'depth'), axis=0, tiled=True)  42.8 us
    dot_general x2, matrix products, row_product_t(): lax.dot_general(left_rows, right_side, (((1,), (1,)), ((), ())), preferre...  42 us
  transfers between devices with their start and end apart: 10, of which 7 were waited for; matrix products, arithmetic and copies ran while one was open for 18% of the time, Pallas kernels for 0%

commit v1 on v0

v1 whole, which is shorter than its diff:
```python
import math

import jax
import jax.numpy as jnp
from jax import lax
from jax.sharding import PartitionSpec as P

root_coeff = math.sqrt(2.0 / math.pi)
CHUNKS = 6
LEAD = 2


def gelu_pair(pre_act):
    inner_arg = root_coeff * (pre_act + 0.044715 * pre_act * pre_act * pre_act)
    tangent = jnp.tanh(inner_arg)
    gelu_value = 0.5 * pre_act * (1.0 + tangent)
    gelu_slope = 0.5 * (1.0 + tangent) + 0.5 * pre_act * (1.0 - tangent * tangent) * root_coeff * (
        1.0 + 0.134145 * pre_act * pre_act
    )
    return (gelu_value, gelu_slope)


def swap(value, axis, mask):
    size = lax.axis_size(axis)
    return lax.ppermute(value, axis, [(i, i ^ mask) for i in range(size)])


def reorder(rows, count, mask):
    height = rows.shape[0] // count
    pieces = [lax.dynamic_slice_in_dim(rows, (i ^ mask) * height, height, 0) for i in range(count)]
    return jnp.concatenate(pieces, axis=0)


def dot_rows(left, right):
    return jnp.dot(left, right, preferred_element_type=jnp.float32)


def dot_rows_t(left, right):
    return lax.dot_general(left, right, (((1,), (1,)), ((), ())), preferred_element_type=jnp.float32)


def dot_tokens(left, right):
    return lax.dot_general(left, right, (((0,), (0,)), ((), ())), preferred_element_type=jnp.float32)


def half(value):
    return value.astype(jnp.bfloat16)


def bits_of(size):
    return [1 << b for b in range(size.bit_length() - 1)]


def gather_tokens(local, depth_at, n_depth, n_cols):
    block = local.shape[0]
    width = local.shape[1] // n_depth
    parts = [
        lax.dynamic_slice_in_dim(local, (depth_at ^ k) * width, width, 1) for k in range(n_depth)
    ]
    parts = [parts[0]] + [swap(parts[k], "depth", k) for k in range(1, n_depth)]
    held = jnp.stack(parts)[None]
    done = 1
    for bit in reversed(bits_of(n_cols)):
        other = swap(held, "col", bit)
        held = jnp.stack([held, other], axis=1).reshape((2 * done,) + held.shape[1:])
        done *= 2
    return held.reshape(n_cols * n_depth * block, width)


def scatter_output(total, n_depth, n_cols, depth_at, beside):
    width = total.shape[1]
    beside = list(beside)
    held = total.reshape(n_cols, -1, width)
    for step, bit in enumerate(bits_of(n_cols)):
        held = held.reshape((held.shape[0] // 2, 2) + held.shape[1:])
        held = held[:, 0] + swap(half(held[:, 1]), "col", bit).astype(jnp.float32)
        if step < len(beside):
            held, beside[step] = lax.optimization_barrier((held, beside[step]))
    mine = half(held[0]).reshape(n_depth, -1, width)
    parts = [mine[0]] + [swap(mine[k], "depth", k) for k in range(1, n_depth)]
    joined = jnp.concatenate(parts, axis=1)
    pieces = [
        lax.dynamic_slice_in_dim(joined, (i ^ depth_at) * width, width, 1) for i in range(n_depth)
    ]
    return jnp.concatenate(pieces, axis=1), beside


class Lane:
    def __init__(self):
        self.ended = []

    def send(self, values, axis, masks):
        if len(self.ended) >= 2:
            values = lax.optimization_barrier((values, self.ended[-2]))[0]
        got = [swap(value, axis, mask) for value, mask in zip(values, masks)]
        self.ended.append(got)
        return got


def body(tokens, w_up, w_down, cotangent):
    depth_at = lax.axis_index("depth")
    n_depth = lax.axis_size("depth")
    n_cols = lax.axis_size("col")
    n_row = lax.axis_size("row")
    owners = n_depth * n_row
    fine = max(owners, n_cols * n_depth)
    owner_at = (depth_at * n_row + lax.axis_index("row")) * (fine // owners)
    token_at = (lax.axis_index("col") * n_depth + depth_at) * (fine // (n_cols * n_depth))
    mask = owner_at ^ token_at
    chunks = max(n for n in (2, 4, 6, 8) if w_up.shape[1] % (n * 128) == 0 and n <= CHUNKS)
    wide = w_up.shape[1] // chunks
    lead = min(LEAD, chunks)

    x_sub = reorder(gather_tokens(tokens, depth_at, n_depth, n_cols), fine, mask)
    cot_sub = reorder(gather_tokens(cotangent, depth_at, n_depth, n_cols), fine, mask)

    ups = [w_up[:, c * wide : (c + 1) * wide] for c in range(chunks)]
    downs = [w_down[c * wide : (c + 1) * wide] for c in range(chunks)]
    span = x_sub.shape[0] // n_depth
    block = span // n_row
    depth_lane, row_lane = Lane(), Lane()
    depth_masks = list(range(1, n_depth))
    row_masks = list(range(1, n_row))

    def make(unit, rows):
        kind, c = unit
        return dot_rows(rows, ups[c]) if kind == "up" else dot_rows_t(rows, downs[c])

    def left(unit):
        return x_sub if unit[0] == "up" else cot_sub

    units = [("up", c) for c in range(lead)]
    for c in range(chunks):
        units.append(("down", c))
        if c + lead < chunks:
            units.append(("up", c + lead))

    count = len(units)
    arrived, mine, column, whole, slopes = {}, {}, {}, {}, {}

    def reduce_depth(unit):
        rows = left(unit)
        away = [half(make(unit, rows[k * span : (k + 1) * span])) for k in depth_masks]
        arrived[unit] = depth_lane.send(away, "depth", depth_masks)

    def reduce_row(unit):
        total = make(unit, left(unit)[:span])
        for piece in arrived[unit]:
            total = total + piece.astype(jnp.float32)
        away = [half(total[k * block : (k + 1) * block]) for k in row_masks]
        result = total[:block]
        for piece in row_lane.send(away, "row", row_masks):
            result = result + piece.astype(jnp.float32)
        if unit[0] == "up":
            gelu_value, slopes[unit[1]] = gelu_pair(result)
            mine[unit] = half(gelu_value)
        else:
            mine[unit] = half(result * slopes[unit[1]])

    def gather_row(unit):
        own = mine[unit]
        got = row_lane.send([own] * len(row_masks), "row", row_masks)
        column[unit] = jnp.concatenate([own] + got, axis=0)

    def gather_depth(unit):
        own = column[unit]
        got = depth_lane.send([own] * len(depth_masks), "depth", depth_masks)
        whole[unit] = jnp.concatenate([own] + got, axis=0)

    for slot in range(count + 3):
        if slot < count:
            reduce_depth(units[slot])
        if 0 <= slot - 1 < count:
            reduce_row(units[slot - 1])
        if 0 <= slot - 2 < count:
            gather_row(units[slot - 2])
        if 0 <= slot - 3 < count:
            gather_depth(units[slot - 3])

    hidden = [whole[("up", c)] for c in range(chunks)]
    d_pre = [whole[("down", c)] for c in range(chunks)]

    def span_of(first, last):
        return slice(first * wide, last * wide)

    middle = chunks // 2
    out_part = dot_rows(jnp.concatenate(hidden[:middle], axis=1), w_down[span_of(0, middle)])
    out_part = out_part + dot_rows(
        jnp.concatenate(hidden[middle:], axis=1), w_down[span_of(middle, chunks)]
    )
    output, _ = scatter_output(reorder(out_part, fine, mask), n_depth, n_cols, depth_at, [])

    dx_part = dot_rows_t(jnp.concatenate(d_pre[:middle], axis=1), w_up[:, span_of(0, middle)])
    dx_part = dx_part + dot_rows_t(
        jnp.concatenate(d_pre[middle:-1], axis=1), w_up[:, span_of(middle, chunks - 1)]
    )
    d_pre[-1], dx_part = lax.optimization_barrier((d_pre[-1], dx_part))
    dx_part = dx_part + dot_rows_t(d_pre[-1], ups[-1])
    ordered = reorder(dx_part, fine, mask)
    hidden_all = jnp.concatenate(hidden, axis=1)
    d_pre_all = jnp.concatenate(d_pre, axis=1)
    ordered, d_pre_all, hidden_all = lax.optimization_barrier((ordered, d_pre_all, hidden_all))
    grad_up = half(dot_tokens(x_sub, d_pre_all))
    grad_down = half(dot_tokens(hidden_all, cot_sub))
    grad_tokens, (grad_up, grad_down) = scatter_output(
        ordered, n_depth, n_cols, depth_at, [grad_up, grad_down]
    )
    return (output, grad_tokens, grad_up, grad_down)


def solution(mesh):
    placed = (
        P(("col", "depth"), "row"),
        P(("row", "depth"), "col"),
        P("col", ("row", "depth")),
        P(("col", "depth"), "row"),
    )
    return jax.shard_map(
        body,
        mesh=mesh,
        in_specs=placed,
        out_specs=(
            P(("col", "depth"), "row"),
            P(("col", "depth"), "row"),
            P(("row", "depth"), "col"),
            P("col", ("row", "depth")),
        ),
        check_vma=False,
    )
```

time: 1140 us -> 721 us (0.63); the launches traced: 1140 us -> 709 us
  waiting for transfers between devices: 914 us -> 256 us
  starting transfers between devices: 7.51 us -> 235 us
  other arithmetic: 54.4 us -> 17.7 us
  local copies, waits for them, and re-layouts: 6.75 us -> 37.3 us
  matrix products: 147 us -> 162 us
  between operations: 14.2 us -> 2.45 us
    reduce_scatter x4 -> x0, waiting for transfers between devices: 614 us -> none  [the longest x1 317 us: body(): lax.psum_scatter(row_product(x_sub, w_up), ('row', 'depth'), scatter_dime...]
    all_gather x4 -> x0, waiting for transfers between devices: 298 us -> none  [the longest x1 137 us: body(): hidden_all = lax.all_gather(hidden, ('row', 'depth'), axis=0, tiled=True)]
    ppermute x0 -> x108, waiting for transfers between devices: none -> 256 us  [swap(): return lax.ppermute(value, axis, [(i, i ^ mask) for i in range(size)])]
    ppermute x0 -> x108, starting transfers between devices: none -> 235 us  [swap(): return lax.ppermute(value, axis, [(i, i ^ mask) for i in range(size)])]
    convert_element_type x5 -> x1, other arithmetic: 54.4 us -> 0.11 us  [half(): return value.astype(jnp.bfloat16)]
    unnamed x2 -> x120, local copies, waits for them, and re-layouts: 1.38 us -> 24.2 us
    dot_general x8 -> x31, matrix products: 147 us -> 162 us  [the longest x14 64 us: dot_rows(): return jnp.dot(left, right, preferred_element_type=jnp.float32)]
  transfers between devices with their start and end apart: 10 -> 108, of which waited for: 7 -> 32; matrix products, arithmetic and copies ran while one was open for 18% -> 27% of each run, Pallas kernels for 0% -> 0%
where the time goes in v1:
time: 721 us; the launch traced here: 709 us
  waiting for transfers between devices  256 us (36%)
  starting transfers between devices  235 us (33%)
  matrix products  162 us (22%)
  local copies, waits for them, and re-layouts  37.3 us (5%)
  other arithmetic  17.7 us (2%)
    ppermute x108, waiting for transfers between devices, swap(): return lax.ppermute(value, axis, [(i, i ^ mask) for i in range(size)])  256 us
    ppermute x108, starting transfers between devices, swap(): return lax.ppermute(value, axis, [(i, i ^ mask) for i in range(size)])  235 us
    dot_general x14, matrix products, dot_rows(): return jnp.dot(left, right, preferred_element_type=jnp.float32)  64 us
    dot_general x15, matrix products, dot_rows_t(): lax.dot_general(left, right, (((1,), (1,)), ((), ())), preferred_element_...  54 us
    dot_general x2, matrix products, dot_tokens(): lax.dot_general(left, right, (((0,), (0,)), ((), ())), preferred_element_...  43.6 us
    unnamed x120, local copies, waits for them, and re-layouts  24.2 us
  transfers between devices with their start and end apart: 108, of which 32 were waited for; matrix products, arithmetic and copies ran while one was open for 27% of the time, Pallas kernels for 0%

profile of v1, /device:TPU:0, one launch (start us, length us, event | category | flops | bytes accessed | tf_op | source)
XLA Modules:
  0.0 709.5 jit_solution(15332267438328199634)
XLA Ops:
  4.8 7.0 collective-permute-done
  15.3 11.1 %collective-permute-done.1 = bf16[1,2,96,1536]{3,2,1,0:T(8,128)(2,1)S(1)} collective-permute-done((bf16[1,2,96,1536]{3,2,1,0:T(8,128)(2,1)S(1)}, bf16[1,2,96,1536]{3,2,1,0:T(8,128)(2,1)S(1)}, u32[]{:S(2)}, u32[]{:S(2)}) %collective-permute-start.1) | collective-permute-done | bytes 589856 | tf_op jit(solution)/shard_map/ppermute | solution.py:25
  29.1 14.5 %collective-permute-done.11 = bf16[1,2,96,1536]{3,2,1,0:T(8,128)(2,1)S(1)} collective-permute-done((bf16[1,2,96,1536]{3,2,1,0:T(8,128)(2,1)}, bf16[1,2,96,1536]{3,2,1,0:T(8,128)(2,1)S(1)}, u32[]{:S(2)}, u32[]{:S(2)}) %collective-permute-start.11) | collective-permute-done | bytes 589856 | tf_op jit(solution)/shard_map/ppermute | solution.py:25
  80.0 13.1 %collective-permute-done.3 = bf16[384,1024]{1,0:T(8,128)(2,1)S(1)} collective-permute-done((bf16[384,1024]{1,0:T(8,128)(2,1)S(1)}, bf16[384,1024]{1,0:T(8,128)(2,1)S(1)}, u32[]{:S(2)}, u32[]{:S(2)}) %collective-permute-start.3) | collective-permute-done | bytes 786464 | tf_op jit(solution)/shard_map/ppermute | solution.py:25
  99.5 10.5 %collective-permute-done.15 = bf16[384,1024]{1,0:T(8,128)(2,1)S(1)} collective-permute-done((bf16[384,1024]{1,0:T(8,128)(2,1)S(1)}, bf16[384,1024]{1,0:T(8,128)(2,1)S(1)}, u32[]{:S(2)}, u32[]{:S(2)}) %collective-permute-start.15) | collective-permute-done | bytes 786464 | tf_op jit(solution)/shard_map/ppermute | solution.py:25
  118.9 7.9 %collective-permute-done.13 = bf16[384,1024]{1,0:T(8,128)(2,1)S(1)} collective-permute-done((bf16[384,1024]{1,0:T(8,128)(2,1)S(1)}, bf16[384,1024]{1,0:T(8,128)(2,1)S(1)}, u32[]{:S(2)}, u32[]{:S(2)}) %collective-permute-start.13) | collective-permute-done | bytes 786464 | tf_op jit(solution)/shard_map/ppermute | solution.py:25
  136.1 11.9 %collective-permute-start.24 = (bf16[96,1024]{1,0:T(8,128)(2,1)S(1)}, bf16[96,1024]{1,0:T(8,128)(2,1)S(1)}, u32[]{:S(2)}, u32[]{:S(2)}) collective-permute-start(bf16[96,1024]{1,0:T(8,128)(2,1)S(1)} %get-tuple-element.111), channel_id=1, source_target_pairs={{0,8},{8,0},{16,24},{24,16},{1,9},{9,1},{17,25},{25,17},{2,10},{10... | collective-permute-start | bytes 589832 | tf_op jit(solution)/shard_map/ppermute | solution.py:25
  156.2 12.4 %collective-permute-done.25 = bf16[96,1024]{1,0:T(8,128)(2,1)S(1)} collective-permute-done((bf16[96,1024]{1,0:T(8,128)(2,1)S(1)}, bf16[96,1024]{1,0:T(8,128)(2,1)S(1)}, u32[]{:S(2)}, u32[]{:S(2)}) %collective-permute-start.25) | collective-permute-done | bytes 196640 | tf_op jit(solution)/shard_map/ppermute | solution.py:25
  177.0 7.0 collective-permute-done.7
  184.0 6.7 collective-permute-done.8
  198.7 13.9 %collective-permute-done.14 = bf16[384,1024]{1,0:T(8,128)(2,1)S(1)} collective-permute-done((bf16[384,1024]{1,0:T(8,128)(2,1)S(1)}, bf16[384,1024]{1,0:T(8,128)(2,1)S(1)}, u32[]{:S(2)}, u32[]{:S(2)}) %collective-permute-start.14) | collective-permute-done | bytes 786464 | tf_op jit(solution)/shard_map/ppermute | solution.py:25
  213.1 9.6 %collective-permute-start.19 = (bf16[96,1024]{1,0:T(8,128)(2,1)S(1)}, bf16[96,1024]{1,0:T(8,128)(2,1)S(1)}, u32[]{:S(2)}, u32[]{:S(2)}) collective-permute-start(bf16[96,1024]{1,0:T(8,128)(2,1)S(1)} %get-tuple-element.108), channel_id=1, source_target_pairs={{0,8},{8,0},{16,24},{24,16},{1,9},{9,1},{17,25},{25,17},{2,10},{10... | collective-permute-start | bytes 589832 | tf_op jit(solution)/shard_map/ppermute | solution.py:25
  230.4 8.0 %collective-permute-done.20 = bf16[96,1024]{1,0:T(8,128)(2,1)S(1)} collective-permute-done((bf16[96,1024]{1,0:T(8,128)(2,1)S(1)}, bf16[96,1024]{1,0:T(8,128)(2,1)S(1)}, u32[]{:S(2)}, u32[]{:S(2)}) %collective-permute-start.20) | collective-permute-done | bytes 196640 | tf_op jit(solution)/shard_map/ppermute | solution.py:25
  238.4 11.0 %collective-permute-start.30 = (bf16[96,1024]{1,0:T(8,128)(2,1)S(1)}, bf16[96,1024]{1,0:T(8,128)(2,1)S(1)}, u32[]{:S(2)}, u32[]{:S(2)}) collective-permute-start(bf16[96,1024]{1,0:T(8,128)(2,1)S(1)} %get-tuple-element.119), channel_id=1, source_target_pairs={{0,8},{8,0},{16,24},{24,16},{1,9},{9,1},{17,25},{25,17},{2,10},{10... | collective-permute-start | bytes 589832 | tf_op jit(solution)/shard_map/ppermute | solution.py:25
  260.7 8.8 %collective-permute-done.31 = bf16[96,1024]{1,0:T(8,128)(2,1)S(1)} collective-permute-done((bf16[96,1024]{1,0:T(8,128)(2,1)S(1)}, bf16[96,1024]{1,0:T(8,128)(2,1)S(1)}, u32[]{:S(2)}, u32[]{:S(2)}) %collective-permute-start.31) | collective-permute-done | bytes 196640 | tf_op jit(solution)/shard_map/ppermute | solution.py:25
  274.1 9.9 %collective-permute-done.54 = bf16[384,1024]{1,0:T(8,128)(2,1)S(1)} collective-permute-done((bf16[384,1024]{1,0:T(8,128)(2,1)S(1)}, bf16[384,1024]{1,0:T(8,128)(2,1)S(1)}, u32[]{:S(2)}, u32[]{:S(2)}) %collective-permute-start.54) | collective-permute-done | bytes 786464 | tf_op jit(solution)/shard_map/ppermute | solution.py:25
  296.1 4.4 collective-permute-done.34
  305.6 10.8 %collective-permute-start.46 = (bf16[96,1024]{1,0:T(8,128)(2,1)S(1)}, bf16[96,1024]{1,0:T(8,128)(2,1)S(1)}, u32[]{:S(2)}, u32[]{:S(2)}) collective-permute-start(bf16[96,1024]{1,0:T(8,128)(2,1)S(1)} %get-tuple-element.135), channel_id=1, source_target_pairs={{0,8},{8,0},{16,24},{24,16},{1,9},{9,1},{17,25},{25,17},{2,10},{10... | collective-permute-start | bytes 589832 | tf_op jit(solution)/shard_map/ppermute | solution.py:25
  324.0 7.4 %collective-permute-start.47 = (bf16[96,1024]{1,0:T(8,128)(2,1)S(1)}, bf16[96,1024]{1,0:T(8,128)(2,1)S(1)}, u32[]{:S(2)}, u32[]{:S(2)}) collective-permute-start(bf16[96,1024]{1,0:T(8,128)(2,1)S(1)} %get-tuple-element.135), channel_id=1, source_target_pairs={{0,16},{8,24},{16,0},{24,8},{1,17},{9,25},{17,1},{25,9},{2,18},{10... | collective-permute-start | bytes 589832 | tf_op jit(solution)/shard_map/ppermute | solution.py:25
  331.5 4.9 collective-permute-start.48
  338.6 5.6 collective-permute-done.48
  346.8 8.1 %collective-permute-done.70 = bf16[384,1024]{1,0:T(8,128)(2,1)S(1)} collective-permute-done((bf16[384,1024]{1,0:T(8,128)(2,1)S(1)}, bf16[384,1024]{1,0:T(8,128)(2,1)S(1)}, u32[]{:S(2)}, u32[]{:S(2)}) %collective-permute-start.70) | collective-permute-done | bytes 786464 | tf_op jit(solution)/shard_map/ppermute | solution.py:25
  364.7 6.0 collective-permute-start.73
  379.1 5.8 collective-permute-start.62
  384.9 11.5 %collective-permute-done.71 = bf16[384,1024]{1,0:T(8,128)(2,1)S(1)} collective-permute-done((bf16[384,1024]{1,0:T(8,128)(2,1)S(1)}, bf16[384,1024]{1,0:T(8,128)(2,1)S(1)}, u32[]{:S(2)}, u32[]{:S(2)}) %collective-permute-start.71) | collective-permute-done | bytes 786464 | tf_op jit(solution)/shard_map/ppermute | solution.py:25
  400.5 4.8 collective-permute-start.63
  413.6 4.7 collective-permute-done.64
  418.2 4.5 collective-permute-start.77
  429.6 11.6 %collective-permute-start.65 = (bf16[96,1024]{1,0:T(8,128)(2,1)S(1)}, bf16[96,1024]{1,0:T(8,128)(2,1)S(1)}, u32[]{:S(2)}, u32[]{:S(2)}) collective-permute-start(bf16[96,1024]{1,0:T(8,128)(2,1)S(1)} %get-tuple-element.154), channel_id=1, source_target_pairs={{0,8},{8,0},{16,24},{24,16},{1,9},{9,1},{17,25},{25,17},{2,10},{10... | collective-permute-start | bytes 589832 | tf_op jit(solution)/shard_map/ppermute | solution.py:25
  449.8 5.1 collective-permute-done.66
  462.7 6.3 collective-permute-done.85
  472.4 7.3 %collective-permute-start.79 = (bf16[96,1024]{1,0:T(8,128)(2,1)S(1)}, bf16[96,1024]{1,0:T(8,128)(2,1)S(1)}, u32[]{:S(2)}, u32[]{:S(2)}) collective-permute-start(bf16[96,1024]{1,0:T(8,128)(2,1)S(1)} %get-tuple-element.167), channel_id=1, source_target_pairs={{0,16},{8,24},{16,0},{24,8},{1,17},{9,25},{17,1},{25,9},{2,18},{10... | collective-permute-start | bytes 589832 | tf_op jit(solution)/shard_map/ppermute | solution.py:25
  492.0 12.6 %collective-permute-done.94 = bf16[96,1024]{1,0:T(8,128)(2,1)S(1)} collective-permute-done((bf16[96,1024]{1,0:T(8,128)(2,1)S(1)}, bf16[96,1024]{1,0:T(8,128)(2,1)S(1)}, u32[]{:S(2)}, u32[]{:S(2)}) %collective-permute-start.94) | collective-permute-done | bytes 196640 | tf_op jit(solution)/shard_map/ppermute | solution.py:25
  505.8 6.1 collective-permute-start.81
  521.9 5.4 collective-permute-start.98
  527.3 4.8 collective-permute-start.86
  533.6 5.5 collective-permute-done.97
  549.9 11.5 %fusion.2 = f32[768,1536]{1,0:T(8,128)} fusion(bf16[6144,1536]{1,0:T(8,128)(2,1)} %param.6, bf16[768,1024]{1,0:T(8,128)(2,1)S(1)} %get-tuple-element.263, bf16[768,1024]{1,0:T(8,128)(2,1)S(1)} %get-tuple-element.288, bf16[768,1024]{1,0:T(8,128)(2,1)S(1)} %get-tuple-element.286), kind=kOutput, calls=%fused_computation.4 | convolution fusion | flops 7261913088 | bytes 18874368 | tf_op jit(solution)/shard_map/dot_general | solution.py:35
  561.5 11.2 %fusion.23 = f32[768,1536]{1,0:T(8,128)S(1)} fusion(f32[768,1536]{1,0:T(8,128)} %fusion.2, bf16[6144,1536]{1,0:T(8,128)(2,1)} %param.6, bf16[768,1024]{1,0:T(8,128)(2,1)S(1)} %copy-done.9, bf16[768,1024]{1,0:T(8,128)(2,1)} %copy-done.13, bf16[768,1024]{1,0:T(8,128)(2,1)S(1)} %copy-done.12), kind=kOutput, calls=%fused_computation.25 | convolution fusion | flops 7263092736 | bytes 23592960 | tf_op jit(solution)/shard_map/dot_general | solution.py:35
  579.4 13.1 %collective-permute-done.104 = bf16[384,1024]{1,0:T(8,128)(2,1)S(1)} collective-permute-done((bf16[384,1024]{1,0:T(8,128)(2,1)S(1)}, bf16[384,1024]{1,0:T(8,128)(2,1)S(1)}, u32[]{:S(2)}, u32[]{:S(2)}) %collective-permute-start.104) | collective-permute-done | bytes 786464 | tf_op jit(solution)/shard_map/ppermute | solution.py:25
  593.5 9.7 %fusion.6 = f32[768,1536]{1,0:T(8,128)} fusion(bf16[1536,6144]{1,0:T(8,128)(2,1)} %param.5, bf16[768,1024]{1,0:T(8,128)(2,1)S(1)} %get-tuple-element.265, bf16[768,1024]{1,0:T(8,128)(2,1)S(1)} %get-tuple-element.272), kind=kOutput, calls=%fused_computation.8 | convolution fusion | flops 4838129664 | bytes 14155776 | tf_op jit(solution)/shard_map/dot_general | solution.py:39
  603.2 13.3 %fusion.28 = f32[768,1536]{1,0:T(8,128)S(1)} fusion(f32[768,1536]{1,0:T(8,128)} %fusion.6, bf16[1536,6144]{1,0:T(8,128)(2,1)} %param.5, bf16[768,1024]{1,0:T(8,128)(2,1)} %copy-done.7, bf16[768,1024]{1,0:T(8,128)(2,1)} %copy-done.10, bf16[768,1024]{1,0:T(8,128)(2,1)} %copy-done.6), kind=kOutput, calls=%fused_computation.26 | convolution fusion | flops 7263092736 | bytes 23592960 | tf_op jit(solution)/shard_map/dot_general | solution.py:39
  617.6 4.5 fusion.80
  626.4 21.7 %convolution_convert_fusion.1 = bf16[1536,6144]{1,0:T(8,128)(2,1)} fusion(bf16[768,1536]{1,0:T(8,128)(2,1)S(1)} %copy-done.3, bf16[768,6144]{1,0:T(8,128)(2,1)} %constant_dynamic-update-slice_fusion.60), kind=kOutput, calls=%fused_computation.1 | convolution fusion | flops 14504951808 | bytes 30670848 | tf_op jit(solution)/shard_map/dot_general | solution.py:43
  648.1 21.9 %convolution_convert_fusion = bf16[6144,1536]{1,0:T(8,128)(2,1)} fusion(bf16[768,6144]{1,0:T(8,128)(2,1)} %get-tuple-element.194, bf16[768,1536]{1,0:T(8,128)(2,1)S(1)} %copy-done.5), kind=kOutput, calls=%fused_computation | convolution fusion | flops 14504951808 | bytes 30670848 | tf_op jit(solution)/shard_map/dot_general | solution.py:43
  674.3 13.8 %collective-permute-done.88 = bf16[1,192,1536]{2,1,0:T(8,128)(2,1)S(1)} collective-permute-done((bf16[1,192,1536]{2,1,0:T(8,128)(2,1)S(1)}, bf16[1,192,1536]{2,1,0:T(8,128)(2,1)S(1)}, u32[]{:S(2)}, u32[]{:S(2)}) %collective-permute-start.88) | collective-permute-done | bytes 589856 | tf_op jit(solution)/shard_map/ppermute | solution.py:25
  690.8 8.1 %collective-permute-done.106 = bf16[1,192,1536]{2,1,0:T(8,128)(2,1)S(1)} collective-permute-done((bf16[1,192,1536]{2,1,0:T(8,128)(2,1)S(1)}, bf16[1,192,1536]{2,1,0:T(8,128)(2,1)S(1)}, u32[]{:S(2)}, u32[]{:S(2)}) %collective-permute-start.106) | collective-permute-done | bytes 589856 | tf_op jit(solution)/shard_map/ppermute | solution.py:25
  701.6 5.4 collective-permute-done.107
  (393 shorter events, 266.2 us)
Async XLA Ops:
  74.2 35.8 %collective-permute-start.15 = (bf16[384,1024]{1,0:T(8,128)(2,1)S(1)}, bf16[384,1024]{1,0:T(8,128)(2,1)S(1)}, u32[]{:S(2)}, u32[]{:S(2)}) collective-permute-start(bf16[384,1024]{1,0:T(8,128)(2,1)S(1)} %fusion.98), channel_id=1, source_target_pairs={{0,1},{1,0},{2,3},{3,2},{4,5},{5,4},{6,7},{7,6},{8,9},{9,8},{10,11... | collective-permute-start | bytes 2359304 | tf_op jit(solution)/shard_map/ppermute | solution.py:25
  93.1 33.7 %collective-permute-start.13 = (bf16[384,1024]{1,0:T(8,128)(2,1)S(1)}, bf16[384,1024]{1,0:T(8,128)(2,1)S(1)}, u32[]{:S(2)}, u32[]{:S(2)}) collective-permute-start(bf16[384,1024]{1,0:T(8,128)(2,1)S(1)} %fusion.95), channel_id=1, source_target_pairs={{0,1},{1,0},{2,3},{3,2},{4,5},{5,4},{6,7},{7,6},{8,9},{9,8},{10,11... | collective-permute-start | bytes 2359304 | tf_op jit(solution)/shard_map/ppermute | solution.py:25
  97.8 55.2 %collective-permute-start.4 = (bf16[96,1024]{1,0:T(8,128)(2,1)S(1)}, bf16[96,1024]{1,0:T(8,128)(2,1)S(1)}, u32[]{:S(2)}, u32[]{:S(2)}) collective-permute-start(bf16[96,1024]{1,0:T(8,128)(2,1)S(1)} %get-tuple-element.317), channel_id=1, source_target_pairs={{0,8},{8,0},{16,24},{24,16},{1,9},{9,1},{17,25},{25,17},{2,10},{10... | collective-permute-start | bytes 589832 | tf_op jit(solution)/shard_map/ppermute | solution.py:25
  109.9 38.1 %collective-permute-start.23 = (bf16[384,1024]{1,0:T(8,128)(2,1)S(1)}, bf16[384,1024]{1,0:T(8,128)(2,1)S(1)}, u32[]{:S(2)}, u32[]{:S(2)}) collective-permute-start(bf16[384,1024]{1,0:T(8,128)(2,1)S(1)} %fusion.101), channel_id=1, source_target_pairs={{0,1},{1,0},{2,3},{3,2},{4,5},{5,4},{6,7},{7,6},{8,9},{9,8},{10,11... | collective-permute-start | bytes 2359304 | tf_op jit(solution)/shard_map/ppermute | solution.py:25
  131.8 22.9 %collective-permute-start.5 = (bf16[96,1024]{1,0:T(8,128)(2,1)S(1)}, bf16[96,1024]{1,0:T(8,128)(2,1)S(1)}, u32[]{:S(2)}, u32[]{:S(2)}) collective-permute-start(bf16[96,1024]{1,0:T(8,128)(2,1)S(1)} %get-tuple-element.319), channel_id=1, source_target_pairs={{0,16},{8,24},{16,0},{24,8},{1,17},{9,25},{17,1},{25,9},{2,18},{10... | collective-permute-start | bytes 589832 | tf_op jit(solution)/shard_map/ppermute | solution.py:25
  131.9 24.3 %collective-permute-start.6 = (bf16[96,1024]{1,0:T(8,128)(2,1)S(1)}, bf16[96,1024]{1,0:T(8,128)(2,1)S(1)}, u32[]{:S(2)}, u32[]{:S(2)}) collective-permute-start(bf16[96,1024]{1,0:T(8,128)(2,1)S(1)} %get-tuple-element.318), channel_id=1, source_target_pairs={{0,24},{8,16},{16,8},{24,0},{1,25},{9,17},{17,9},{25,1},{2,26},{10... | collective-permute-start | bytes 589832 | tf_op jit(solution)/shard_map/ppermute | solution.py:25
  154.7 40.2 %collective-permute-start.38 = (bf16[384,1024]{1,0:T(8,128)(2,1)S(1)}, bf16[384,1024]{1,0:T(8,128)(2,1)S(1)}, u32[]{:S(2)}, u32[]{:S(2)}) collective-permute-start(bf16[384,1024]{1,0:T(8,128)(2,1)S(1)} %fusion.107), channel_id=1, source_target_pairs={{0,1},{1,0},{2,3},{3,2},{4,5},{5,4},{6,7},{7,6},{8,9},{9,8},{10,11... | collective-permute-start | bytes 2359304 | tf_op jit(solution)/shard_map/ppermute | solution.py:25
  175.9 46.7 %collective-permute-start.27 = (bf16[96,1024]{1,0:T(8,128)(2,1)S(1)}, bf16[96,1024]{1,0:T(8,128)(2,1)S(1)}, u32[]{:S(2)}, u32[]{:S(2)}) collective-permute-start(bf16[96,1024]{1,0:T(8,128)(2,1)S(1)} %get-tuple-element.114), channel_id=1, source_target_pairs={{0,8},{8,0},{16,24},{24,16},{1,9},{9,1},{17,25},{25,17},{2,10},{10... | collective-permute-start | bytes 589832 | tf_op jit(solution)/shard_map/ppermute | solution.py:25
  184.0 38.6 %collective-permute-start.28 = (bf16[96,1024]{1,0:T(8,128)(2,1)S(1)}, bf16[96,1024]{1,0:T(8,128)(2,1)S(1)}, u32[]{:S(2)}, u32[]{:S(2)}) collective-permute-start(bf16[96,1024]{1,0:T(8,128)(2,1)S(1)} %get-tuple-element.115), channel_id=1, source_target_pairs={{0,16},{8,24},{16,0},{24,8},{1,17},{9,25},{17,1},{25,9},{2,18},{10... | collective-permute-start | bytes 589832 | tf_op jit(solution)/shard_map/ppermute | solution.py:25
  190.7 34.4 %collective-permute-start.29 = (bf16[96,1024]{1,0:T(8,128)(2,1)S(1)}, bf16[96,1024]{1,0:T(8,128)(2,1)S(1)}, u32[]{:S(2)}, u32[]{:S(2)}) collective-permute-start(bf16[96,1024]{1,0:T(8,128)(2,1)S(1)} %get-tuple-element.116), channel_id=1, source_target_pairs={{0,24},{8,16},{16,8},{24,0},{1,25},{9,17},{17,9},{25,1},{2,26},{10... | collective-permute-start | bytes 589832 | tf_op jit(solution)/shard_map/ppermute | solution.py:25
  194.8 54.8 %collective-permute-start.39 = (bf16[384,1024]{1,0:T(8,128)(2,1)S(1)}, bf16[384,1024]{1,0:T(8,128)(2,1)S(1)}, u32[]{:S(2)}, u32[]{:S(2)}) collective-permute-start(bf16[384,1024]{1,0:T(8,128)(2,1)S(1)} %fusion.104), channel_id=1, source_target_pairs={{0,1},{1,0},{2,3},{3,2},{4,5},{5,4},{6,7},{7,6},{8,9},{9,8},{10,11... | collective-permute-start | bytes 2359304 | tf_op jit(solution)/shard_map/ppermute | solution.py:25
  225.1 30.2 %collective-permute-start.40 = (bf16[96,1024]{1,0:T(8,128)(2,1)S(1)}, bf16[96,1024]{1,0:T(8,128)(2,1)S(1)}, u32[]{:S(2)}, u32[]{:S(2)}) collective-permute-start(bf16[96,1024]{1,0:T(8,128)(2,1)S(1)} %get-tuple-element.127), channel_id=1, source_target_pairs={{0,8},{8,0},{16,24},{24,16},{1,9},{9,1},{17,25},{25,17},{2,10},{10... | collective-permute-start | bytes 589832 | tf_op jit(solution)/shard_map/ppermute | solution.py:25
  230.0 25.6 %collective-permute-start.41 = (bf16[96,1024]{1,0:T(8,128)(2,1)S(1)}, bf16[96,1024]{1,0:T(8,128)(2,1)S(1)}, u32[]{:S(2)}, u32[]{:S(2)}) collective-permute-start(bf16[96,1024]{1,0:T(8,128)(2,1)S(1)} %get-tuple-element.128), channel_id=1, source_target_pairs={{0,16},{8,24},{16,0},{24,8},{1,17},{9,25},{17,1},{25,9},{2,18},{10... | collective-permute-start | bytes 589832 | tf_op jit(solution)/shard_map/ppermute | solution.py:25
  249.6 22.0 %collective-permute-start.22 = (bf16[384,1024]{1,0:T(8,128)(2,1)S(1)}, bf16[384,1024]{1,0:T(8,128)(2,1)S(1)}, u32[]{:S(2)}, u32[]{:S(2)}) collective-permute-start(bf16[384,1024]{1,0:T(8,128)(2,1)S(1)} %pad_maximum_fusion.9), channel_id=1, source_target_pairs={{0,1},{1,0},{2,3},{3,2},{4,5},{5,4},{6,7},{7,6},{8,9},{9,8},{10,11... | collective-permute-start | bytes 2359304 | tf_op jit(solution)/shard_map/ppermute | solution.py:25
  257.9 29.6 %collective-permute-start.43 = (bf16[96,1024]{1,0:T(8,128)(2,1)S(1)}, bf16[96,1024]{1,0:T(8,128)(2,1)S(1)}, u32[]{:S(2)}, u32[]{:S(2)}) collective-permute-start(bf16[96,1024]{1,0:T(8,128)(2,1)S(1)} %get-tuple-element.130), channel_id=1, source_target_pairs={{0,8},{8,0},{16,24},{24,16},{1,9},{9,1},{17,25},{25,17},{2,10},{10... | collective-permute-start | bytes 589832 | tf_op jit(solution)/shard_map/ppermute | solution.py:25
  260.0 29.9 %collective-permute-start.44 = (bf16[96,1024]{1,0:T(8,128)(2,1)S(1)}, bf16[96,1024]{1,0:T(8,128)(2,1)S(1)}, u32[]{:S(2)}, u32[]{:S(2)}) collective-permute-start(bf16[96,1024]{1,0:T(8,128)(2,1)S(1)} %get-tuple-element.131), channel_id=1, source_target_pairs={{0,16},{8,24},{16,0},{24,8},{1,17},{9,25},{17,1},{25,9},{2,18},{10... | collective-permute-start | bytes 589832 | tf_op jit(solution)/shard_map/ppermute | solution.py:25
  270.2 21.9 %collective-permute-start.45 = (bf16[96,1024]{1,0:T(8,128)(2,1)S(1)}, bf16[96,1024]{1,0:T(8,128)(2,1)S(1)}, u32[]{:S(2)}, u32[]{:S(2)}) collective-permute-start(bf16[96,1024]{1,0:T(8,128)(2,1)S(1)} %get-tuple-element.132), channel_id=1, source_target_pairs={{0,24},{8,16},{16,8},{24,0},{1,25},{9,17},{17,9},{25,1},{2,26},{10... | collective-permute-start | bytes 589832 | tf_op jit(solution)/shard_map/ppermute | solution.py:25
  271.6 31.8 %collective-permute-start.36 = (bf16[384,1024]{1,0:T(8,128)(2,1)S(1)}, bf16[384,1024]{1,0:T(8,128)(2,1)S(1)}, u32[]{:S(2)}, u32[]{:S(2)}) collective-permute-start(bf16[384,1024]{1,0:T(8,128)(2,1)S(1)} %pad_maximum_fusion.11), channel_id=1, source_target_pairs={{0,1},{1,0},{2,3},{3,2},{4,5},{5,4},{6,7},{7,6},{8,9},{9,8},{10,11... | collective-permute-start | bytes 2359304 | tf_op jit(solution)/shard_map/ppermute | solution.py:25
  292.1 31.9 %collective-permute-start.56 = (bf16[96,1024]{1,0:T(8,128)(2,1)S(1)}, bf16[96,1024]{1,0:T(8,128)(2,1)S(1)}, u32[]{:S(2)}, u32[]{:S(2)}) collective-permute-start(bf16[96,1024]{1,0:T(8,128)(2,1)S(1)} %get-tuple-element.143), channel_id=1, source_target_pairs={{0,8},{8,0},{16,24},{24,16},{1,9},{9,1},{17,25},{25,17},{2,10},{10... | collective-permute-start | bytes 589832 | tf_op jit(solution)/shard_map/ppermute | solution.py:25
  296.1 35.4 %collective-permute-start.57 = (bf16[96,1024]{1,0:T(8,128)(2,1)S(1)}, bf16[96,1024]{1,0:T(8,128)(2,1)S(1)}, u32[]{:S(2)}, u32[]{:S(2)}) collective-permute-start(bf16[96,1024]{1,0:T(8,128)(2,1)S(1)} %get-tuple-element.144), channel_id=1, source_target_pairs={{0,16},{8,24},{16,0},{24,8},{1,17},{9,25},{17,1},{25,9},{2,18},{10... | collective-permute-start | bytes 589832 | tf_op jit(solution)/shard_map/ppermute | solution.py:25
  300.6 35.9 %collective-permute-start.58 = (bf16[96,1024]{1,0:T(8,128)(2,1)S(1)}, bf16[96,1024]{1,0:T(8,128)(2,1)S(1)}, u32[]{:S(2)}, u32[]{:S(2)}) collective-permute-start(bf16[96,1024]{1,0:T(8,128)(2,1)S(1)} %get-tuple-element.145), channel_id=1, source_target_pairs={{0,24},{8,16},{16,8},{24,0},{1,25},{9,17},{17,9},{25,1},{2,26},{10... | collective-permute-start | bytes 589832 | tf_op jit(solution)/shard_map/ppermute | solution.py:25
  305.6 30.9 %collective-permute-start.46 = (bf16[96,1024]{1,0:T(8,128)(2,1)S(1)}, bf16[96,1024]{1,0:T(8,128)(2,1)S(1)}, u32[]{:S(2)}, u32[]{:S(2)}) collective-permute-start(bf16[96,1024]{1,0:T(8,128)(2,1)S(1)} %get-tuple-element.135), channel_id=1, source_target_pairs={{0,8},{8,0},{16,24},{24,16},{1,9},{9,1},{17,25},{25,17},{2,10},{10... | collective-permute-start | bytes 589832 | tf_op jit(solution)/shard_map/ppermute | solution.py:25
  320.5 24.6 %collective-permute-start.37 = (bf16[384,1024]{1,0:T(8,128)(2,1)S(1)}, bf16[384,1024]{1,0:T(8,128)(2,1)S(1)}, u32[]{:S(2)}, u32[]{:S(2)}) collective-permute-start(bf16[384,1024]{1,0:T(8,128)(2,1)S(1)} %pad_maximum_fusion.10), channel_id=1, source_target_pairs={{0,1},{1,0},{2,3},{3,2},{4,5},{5,4},{6,7},{7,6},{8,9},{9,8},{10,11... | collective-permute-start | bytes 2359304 | tf_op jit(solution)/shard_map/ppermute | solution.py:25
  336.5 24.5 %collective-permute-start.59 = (bf16[96,1024]{1,0:T(8,128)(2,1)S(1)}, bf16[96,1024]{1,0:T(8,128)(2,1)S(1)}, u32[]{:S(2)}, u32[]{:S(2)}) collective-permute-start(bf16[96,1024]{1,0:T(8,128)(2,1)S(1)} %get-tuple-element.146), channel_id=1, source_target_pairs={{0,8},{8,0},{16,24},{24,16},{1,9},{9,1},{17,25},{25,17},{2,10},{10... | collective-permute-start | bytes 589832 | tf_op jit(solution)/shard_map/ppermute | solution.py:25
  336.5 24.7 %collective-permute-start.60 = (bf16[96,1024]{1,0:T(8,128)(2,1)S(1)}, bf16[96,1024]{1,0:T(8,128)(2,1)S(1)}, u32[]{:S(2)}, u32[]{:S(2)}) collective-permute-start(bf16[96,1024]{1,0:T(8,128)(2,1)S(1)} %get-tuple-element.147), channel_id=1, source_target_pairs={{0,16},{8,24},{16,0},{24,8},{1,17},{9,25},{17,1},{25,9},{2,18},{10... | collective-permute-start | bytes 589832 | tf_op jit(solution)/shard_map/ppermute | solution.py:25
  345.1 31.7 %collective-permute-start.52 = (bf16[384,1024]{1,0:T(8,128)(2,1)S(1)}, bf16[384,1024]{1,0:T(8,128)(2,1)S(1)}, u32[]{:S(2)}, u32[]{:S(2)}) collective-permute-start(bf16[384,1024]{1,0:T(8,128)(2,1)S(1)} %pad_maximum_fusion.13), channel_id=1, source_target_pairs={{0,1},{1,0},{2,3},{3,2},{4,5},{5,4},{6,7},{7,6},{8,9},{9,8},{10,11... | collective-permute-start | bytes 2359304 | tf_op jit(solution)/shard_map/ppermute | solution.py:25
  363.6 36.9 %collective-permute-start.72 = (bf16[96,1024]{1,0:T(8,128)(2,1)S(1)}, bf16[96,1024]{1,0:T(8,128)(2,1)S(1)}, u32[]{:S(2)}, u32[]{:S(2)}) collective-permute-start(bf16[96,1024]{1,0:T(8,128)(2,1)S(1)} %get-tuple-element.159), channel_id=1, source_target_pairs={{0,8},{8,0},{16,24},{24,16},{1,9},{9,1},{17,25},{25,17},{2,10},{10... | collective-permute-start | bytes 589832 | tf_op jit(solution)/shard_map/ppermute | solution.py:25
  364.7 40.7 %collective-permute-start.73 = (bf16[96,1024]{1,0:T(8,128)(2,1)S(1)}, bf16[96,1024]{1,0:T(8,128)(2,1)S(1)}, u32[]{:S(2)}, u32[]{:S(2)}) collective-permute-start(bf16[96,1024]{1,0:T(8,128)(2,1)S(1)} %get-tuple-element.160), channel_id=1, source_target_pairs={{0,16},{8,24},{16,0},{24,8},{1,17},{9,25},{17,1},{25,9},{2,18},{10... | collective-permute-start | bytes 589832 | tf_op jit(solution)/shard_map/ppermute | solution.py:25
  373.5 35.3 %collective-permute-start.74 = (bf16[96,1024]{1,0:T(8,128)(2,1)S(1)}, bf16[96,1024]{1,0:T(8,128)(2,1)S(1)}, u32[]{:S(2)}, u32[]{:S(2)}) collective-permute-start(bf16[96,1024]{1,0:T(8,128)(2,1)S(1)} %get-tuple-element.161), channel_id=1, source_target_pairs={{0,24},{8,16},{16,8},{24,0},{1,25},{9,17},{17,9},{25,1},{2,26},{10... | collective-permute-start | bytes 589832 | tf_op jit(solution)/shard_map/ppermute | solution.py:25
  379.1 31.6 %collective-permute-start.62 = (bf16[96,1024]{1,0:T(8,128)(2,1)S(1)}, bf16[96,1024]{1,0:T(8,128)(2,1)S(1)}, u32[]{:S(2)}, u32[]{:S(2)}) collective-permute-start(bf16[96,1024]{1,0:T(8,128)(2,1)S(1)} %get-tuple-element.151), channel_id=1, source_target_pairs={{0,8},{8,0},{16,24},{24,16},{1,9},{9,1},{17,25},{25,17},{2,10},{10... | collective-permute-start | bytes 589832 | tf_op jit(solution)/shard_map/ppermute | solution.py:25
  396.4 27.0 %collective-permute-start.53 = (bf16[384,1024]{1,0:T(8,128)(2,1)S(1)}, bf16[384,1024]{1,0:T(8,128)(2,1)S(1)}, u32[]{:S(2)}, u32[]{:S(2)}) collective-permute-start(bf16[384,1024]{1,0:T(8,128)(2,1)S(1)} %pad_maximum_fusion.12), channel_id=1, source_target_pairs={{0,1},{1,0},{2,3},{3,2},{4,5},{5,4},{6,7},{7,6},{8,9},{9,8},{10,11... | collective-permute-start | bytes 2359304 | tf_op jit(solution)/shard_map/ppermute | solution.py:25
  410.7 33.8 %collective-permute-start.75 = (bf16[96,1024]{1,0:T(8,128)(2,1)S(1)}, bf16[96,1024]{1,0:T(8,128)(2,1)S(1)}, u32[]{:S(2)}, u32[]{:S(2)}) collective-permute-start(bf16[96,1024]{1,0:T(8,128)(2,1)S(1)} %get-tuple-element.162), channel_id=1, source_target_pairs={{0,8},{8,0},{16,24},{24,16},{1,9},{9,1},{17,25},{25,17},{2,10},{10... | collective-permute-start | bytes 589832 | tf_op jit(solution)/shard_map/ppermute | solution.py:25
  411.4 33.2 %collective-permute-start.76 = (bf16[96,1024]{1,0:T(8,128)(2,1)S(1)}, bf16[96,1024]{1,0:T(8,128)(2,1)S(1)}, u32[]{:S(2)}, u32[]{:S(2)}) collective-permute-start(bf16[96,1024]{1,0:T(8,128)(2,1)S(1)} %get-tuple-element.163), channel_id=1, source_target_pairs={{0,16},{8,24},{16,0},{24,8},{1,17},{9,25},{17,1},{25,9},{2,18},{10... | collective-permute-start | bytes 589832 | tf_op jit(solution)/shard_map/ppermute | solution.py:25
  418.2 28.8 %collective-permute-start.77 = (bf16[96,1024]{1,0:T(8,128)(2,1)S(1)}, bf16[96,1024]{1,0:T(8,128)(2,1)S(1)}, u32[]{:S(2)}, u32[]{:S(2)}) collective-permute-start(bf16[96,1024]{1,0:T(8,128)(2,1)S(1)} %get-tuple-element.164), channel_id=1, source_target_pairs={{0,24},{8,16},{16,8},{24,0},{1,25},{9,17},{17,9},{25,1},{2,26},{10... | collective-permute-start | bytes 589832 | tf_op jit(solution)/shard_map/ppermute | solution.py:25
  423.5 34.4 %collective-permute-start.68 = (bf16[384,1024]{1,0:T(8,128)(2,1)S(1)}, bf16[384,1024]{1,0:T(8,128)(2,1)S(1)}, u32[]{:S(2)}, u32[]{:S(2)}) collective-permute-start(bf16[384,1024]{1,0:T(8,128)(2,1)S(1)} %pad_maximum_fusion.15), channel_id=1, source_target_pairs={{0,1},{1,0},{2,3},{3,2},{4,5},{5,4},{6,7},{7,6},{8,9},{9,8},{10,11... | collective-permute-start | bytes 2359304 | tf_op jit(solution)/shard_map/ppermute | solution.py:25
  447.0 25.3 %collective-permute-start.90 = (bf16[96,1024]{1,0:T(8,128)(2,1)S(1)}, bf16[96,1024]{1,0:T(8,128)(2,1)S(1)}, u32[]{:S(2)}, u32[]{:S(2)}) collective-permute-start(bf16[96,1024]{1,0:T(8,128)(2,1)S(1)} %get-tuple-element.174), channel_id=1, source_target_pairs={{0,8},{8,0},{16,24},{24,16},{1,9},{9,1},{17,25},{25,17},{2,10},{10... | collective-permute-start | bytes 589832 | tf_op jit(solution)/shard_map/ppermute | solution.py:25
  448.1 31.6 %collective-permute-start.91 = (bf16[96,1024]{1,0:T(8,128)(2,1)S(1)}, bf16[96,1024]{1,0:T(8,128)(2,1)S(1)}, u32[]{:S(2)}, u32[]{:S(2)}) collective-permute-start(bf16[96,1024]{1,0:T(8,128)(2,1)S(1)} %get-tuple-element.175), channel_id=1, source_target_pairs={{0,16},{8,24},{16,0},{24,8},{1,17},{9,25},{17,1},{25,9},{2,18},{10... | collective-permute-start | bytes 589832 | tf_op jit(solution)/shard_map/ppermute | solution.py:25
  454.9 26.4 %collective-permute-start.92 = (bf16[96,1024]{1,0:T(8,128)(2,1)S(1)}, bf16[96,1024]{1,0:T(8,128)(2,1)S(1)}, u32[]{:S(2)}, u32[]{:S(2)}) collective-permute-start(bf16[96,1024]{1,0:T(8,128)(2,1)S(1)} %get-tuple-element.176), channel_id=1, source_target_pairs={{0,24},{8,16},{16,8},{24,0},{1,25},{9,17},{17,9},{25,1},{2,26},{10... | collective-permute-start | bytes 589832 | tf_op jit(solution)/shard_map/ppermute | solution.py:25
  469.0 21.8 %collective-permute-start.69 = (bf16[384,1024]{1,0:T(8,128)(2,1)S(1)}, bf16[384,1024]{1,0:T(8,128)(2,1)S(1)}, u32[]{:S(2)}, u32[]{:S(2)}) collective-permute-start(bf16[384,1024]{1,0:T(8,128)(2,1)S(1)} %pad_maximum_fusion.14), channel_id=1, source_target_pairs={{0,1},{1,0},{2,3},{3,2},{4,5},{5,4},{6,7},{7,6},{8,9},{9,8},{10,11... | collective-permute-start | bytes 2359304 | tf_op jit(solution)/shard_map/ppermute | solution.py:25
  481.4 23.2 %collective-permute-start.94 = (bf16[96,1024]{1,0:T(8,128)(2,1)S(1)}, bf16[96,1024]{1,0:T(8,128)(2,1)S(1)}, u32[]{:S(2)}, u32[]{:S(2)}) collective-permute-start(bf16[96,1024]{1,0:T(8,128)(2,1)S(1)} %get-tuple-element.178), channel_id=1, source_target_pairs={{0,16},{8,24},{16,0},{24,8},{1,17},{9,25},{17,1},{25,9},{2,18},{10... | collective-permute-start | bytes 589832 | tf_op jit(solution)/shard_map/ppermute | solution.py:25
  516.1 24.8 %collective-permute-start.100 = (bf16[384,1024]{1,0:T(8,128)(2,1)S(1)}, bf16[384,1024]{1,0:T(8,128)(2,1)S(1)}, u32[]{:S(2)}, u32[]{:S(2)}) collective-permute-start(bf16[384,1024]{1,0:T(8,128)(2,1)S(1)} %pad_maximum_fusion.18), channel_id=1, source_target_pairs={{0,1},{1,0},{2,3},{3,2},{4,5},{5,4},{6,7},{7,6},{8,9},{9,8},{10,11... | collective-permute-start | bytes 2359304 | tf_op jit(solution)/shard_map/ppermute | solution.py:25
  543.0 30.2 %collective-permute-start.101 = (bf16[96,1024]{1,0:T(8,128)(2,1)S(1)}, bf16[96,1024]{1,0:T(8,128)(2,1)S(1)}, u32[]{:S(2)}, u32[]{:S(2)}) collective-permute-start(bf16[96,1024]{1,0:T(8,128)(2,1)S(1)} %get-tuple-element.187), channel_id=1, source_target_pairs={{0,8},{8,0},{16,24},{24,16},{1,9},{9,1},{17,25},{25,17},{2,10},{10... | collective-permute-start | bytes 589832 | tf_op jit(solution)/shard_map/ppermute | solution.py:25
  545.8 27.4 %collective-permute-start.102 = (bf16[96,1024]{1,0:T(8,128)(2,1)S(1)}, bf16[96,1024]{1,0:T(8,128)(2,1)S(1)}, u32[]{:S(2)}, u32[]{:S(2)}) collective-permute-start(bf16[96,1024]{1,0:T(8,128)(2,1)S(1)} %get-tuple-element.187), channel_id=1, source_target_pairs={{0,16},{8,24},{16,0},{24,8},{1,17},{9,25},{17,1},{25,9},{2,18},{10... | collective-permute-start | bytes 589832 | tf_op jit(solution)/shard_map/ppermute | solution.py:25
  547.3 25.9 %collective-permute-start.103 = (bf16[96,1024]{1,0:T(8,128)(2,1)S(1)}, bf16[96,1024]{1,0:T(8,128)(2,1)S(1)}, u32[]{:S(2)}, u32[]{:S(2)}) collective-permute-start(bf16[96,1024]{1,0:T(8,128)(2,1)S(1)} %get-tuple-element.187), channel_id=1, source_target_pairs={{0,24},{8,16},{16,8},{24,0},{1,25},{9,17},{17,9},{25,1},{2,26},{10... | collective-permute-start | bytes 589832 | tf_op jit(solution)/shard_map/ppermute | solution.py:25
  577.0 93.1 %collective-permute-start.87 = (bf16[2,192,1536]{2,1,0:T(8,128)(2,1)}, bf16[2,192,1536]{2,1,0:T(8,128)(2,1)}, u32[]{:S(2)}, u32[]{:S(2)}) collective-permute-start(bf16[2,192,1536]{2,1,0:T(8,128)(2,1)} %fusion.125), channel_id=1, source_target_pairs={{0,2},{2,0},{4,6},{6,4},{1,3},{3,1},{5,7},{7,5},{8,10},{10,8},{12,... | collective-permute-start | bytes 3538952 | tf_op jit(solution)/shard_map/ppermute | solution.py:25
  577.0 39.5 %collective-permute-start.99 = (bf16[384,1024]{1,0:T(8,128)(2,1)}, bf16[384,1024]{1,0:T(8,128)(2,1)}, u32[]{:S(2)}, u32[]{:S(2)}) collective-permute-start(bf16[384,1024]{1,0:T(8,128)(2,1)} %pad_maximum_fusion.17), channel_id=1, source_target_pairs={{0,1},{1,0},{2,3},{3,2},{4,5},{5,4},{6,7},{7,6},{8,9},{9,8},{10,11... | collective-permute-start | bytes 2359304 | tf_op jit(solution)/shard_map/ppermute | solution.py:25
  625.0 46.8 %collective-permute-start.105 = (bf16[2,192,1536]{2,1,0:T(8,128)(2,1)S(1)}, bf16[2,192,1536]{2,1,0:T(8,128)(2,1)S(1)}, u32[]{:S(2)}, u32[]{:S(2)}) collective-permute-start(bf16[2,192,1536]{2,1,0:T(8,128)(2,1)S(1)} %fusion.126), channel_id=1, source_target_pairs={{0,2},{2,0},{4,6},{6,4},{1,3},{3,1},{5,7},{7,5},{8,10},{10,8},{12,... | collective-permute-start | bytes 3538952 | tf_op jit(solution)/shard_map/ppermute | solution.py:25
  672.3 26.6 %collective-permute-start.106 = (bf16[1,192,1536]{2,1,0:T(8,128)(2,1)S(1)}, bf16[1,192,1536]{2,1,0:T(8,128)(2,1)S(1)}, u32[]{:S(2)}, u32[]{:S(2)}) collective-permute-start(bf16[1,192,1536]{2,1,0:T(8,128)(2,1)S(1)} %fusion.135), channel_id=1, source_target_pairs={{0,4},{2,6},{4,0},{6,2},{1,5},{3,7},{5,1},{7,3},{8,12},{10,14},{12... | collective-permute-start | bytes 1769480 | tf_op jit(solution)/shard_map/ppermute | solution.py:25
  (82 other events, 1204.5 us)
